TPU v7x, 256 devices: a whole 4x4x8 slice. The times are simulated.
256 devices in a mesh: row: 16 (over y, z_lo, core), sample: 16 (over z_hi, x).
Axes of the slice: x: 4, y: 4, z: 8 (z_hi: 4, z_lo: 2; z = z_hi * 2 + z_lo), core: 2. Of those that a mesh axis runs over, the one named last changes fastest.
Arguments:
- atom_feat: bfloat16 [32, 18432, 128], P('sample', 'row'), may hold values from -24 to 24
- atom_token: int32 [18432], P('row'), may hold values from 0 to 1151, as said below
- pair_cond: bfloat16 [1152, 1152, 128], P('row', 'sample'), may hold values from -24 to 24
- token_mask: int32 [1152], P('sample'), may hold values 0 or 1
- atom_wq: bfloat16 [128, 128], replicated, may hold values from -3 to 3
- atom_wk: bfloat16 [128, 128], replicated, may hold values from -3 to 3
- atom_wv: bfloat16 [128, 128], replicated, may hold values from -0.5 to 0.5
- atom_wo: bfloat16 [128, 128], replicated, may hold values from -0.5 to 0.5
- agg_weight: bfloat16 [128, 768], replicated, may hold values from -0.5 to 0.5
- pair_weight: bfloat16 [128, 16], replicated, may hold values from -64 to 64
- token_gain: float32 [768], replicated, may hold values from 0.5 to 1.5
- query_weight: bfloat16 [768, 768], replicated, may hold values from -0.21875 to 0.21875
- key_weight: bfloat16 [768, 768], replicated, may hold values from -0.21875 to 0.21875
- value_weight: bfloat16 [768, 768], replicated, may hold values from -0.21875 to 0.21875
- gate_weight: bfloat16 [768, 768], replicated, may hold values from -0.21875 to 0.21875
- out_weight: bfloat16 [768, 768], replicated, may hold values from -0.21875 to 0.21875
Outputs:
- token_out: bfloat16 [32, 1152, 768], P('sample', 'row')
Inputs may be any that keep to these rules, and one draw needn't show every extreme that they name: atom_token never falls along the atoms; atoms 1152 r to 1152 (r + 1) - 1 belong to tokens 72 r to 72 (r + 1) - 1, and every token has at least one atom.
All inputs are finite; a program needn't handle non-finite values. No bound on the sum of `token_mask` on one device may be relied on, other than what follows from the above.
Results may differ from a plain program's by a relative error of at most 0.008.
The roundings to bfloat16 on the way count: a program that leaves them out, or rounds other values in their place, can miss the bound.
Values may be sent and summed in bfloat16 or wider, within the bound.
A program may use at most 128 MiB of HBM per device.

v0:
```python
import jax
import jax.numpy as jnp
from jax import lax
from jax.sharding import PartitionSpec as P

HEADS = 16
HEAD_DIM = 48
AHEADS = 4
AHEAD_DIM = 32
QWIN = 32
KWIN = 128


def with_halo(shard, sides, width):
    for axis, dim in sides:
        devices, length = (lax.axis_size(axis), shard.shape[dim])
        up = [(i, (i + 1) % devices) for i in range(devices - 1)]
        down = [(j, i) for i, j in up]
        last = lax.slice_in_dim(shard, length - width, length, axis=dim)
        leading = lax.slice_in_dim(shard, 0, width, axis=dim)
        before = lax.ppermute(last, axis, up)
        after = lax.ppermute(leading, axis, down)
        shard = jnp.concatenate([before, shard, after], axis=dim)
    return shard


def layer_norm(x):
    mean = jnp.mean(x, -1, keepdims=True)
    centre = x - mean
    var = jnp.mean(centre * centre, -1, keepdims=True)
    return centre * lax.rsqrt(var + 1e-05)


def shards(
    atom_feat,
    atom_token,
    pair_cond,
    token_mask,
    atom_wq,
    atom_wk,
    atom_wv,
    atom_wo,
    agg_weight,
    pair_weight,
    token_gain,
    query_weight,
    key_weight,
    value_weight,
    gate_weight,
    out_weight,
):
    samples, atoms, chans = atom_feat.shape
    rim = (KWIN - QWIN) // 2
    windows = atoms // QWIN
    row_rank = lax.axis_index("row")
    all_atoms = atoms * lax.axis_size("row")
    normed = layer_norm(atom_feat.astype(jnp.float32)).astype(jnp.bfloat16)
    query = jnp.dot(normed, atom_wq, preferred_element_type=jnp.float32).astype(jnp.bfloat16)
    padded = with_halo(normed, (("row", 1),), rim)
    keys_pad = jnp.dot(padded, atom_wk, preferred_element_type=jnp.float32).astype(jnp.bfloat16)
    vals_pad = jnp.dot(padded, atom_wv, preferred_element_type=jnp.float32).astype(jnp.bfloat16)
    keys_pad = keys_pad.reshape(samples, windows + 3, QWIN, chans)
    vals_pad = vals_pad.reshape(samples, windows + 3, QWIN, chans)
    akeys = jnp.concatenate([keys_pad[:, k : k + windows] for k in range(4)], axis=2).reshape(
        samples, windows, KWIN, AHEADS, AHEAD_DIM
    )
    avals = jnp.concatenate([vals_pad[:, k : k + windows] for k in range(4)], axis=2).reshape(
        samples, windows, KWIN, AHEADS, AHEAD_DIM
    )
    aquery = query.reshape(samples, windows, QWIN, AHEADS, AHEAD_DIM)
    wid = jnp.arange(windows, dtype=jnp.int32)
    tid = jnp.arange(KWIN, dtype=jnp.int32)
    gidx = row_rank * atoms - rim + wid[:, None] * QWIN + tid[None, :]
    valid = (gidx >= 0) & (gidx < all_atoms)
    ascores = jnp.einsum(
        "swqhd,swkhd->swhqk", aquery, akeys, preferred_element_type=jnp.float32
    ) * (1.0 / AHEAD_DIM**0.5)
    ascores = jnp.where(valid[None, :, None, None, :], ascores, -jnp.inf)
    aexp = jnp.exp(ascores - jnp.max(ascores, -1, keepdims=True))
    atotal = jnp.sum(aexp, -1)
    amix = (
        jnp.einsum(
            "swhqk,swkhd->swhqd",
            aexp.astype(jnp.bfloat16),
            avals,
            preferred_element_type=jnp.float32,
        )
        / atotal[..., None]
    )
    amix = jnp.transpose(amix, (0, 1, 3, 2, 4)).reshape(samples, atoms, chans).astype(jnp.bfloat16)
    atom_out = (
        atom_feat.astype(jnp.float32) + jnp.dot(amix, atom_wo, preferred_element_type=jnp.float32)
    ).astype(jnp.bfloat16)
    hidden = jax.nn.relu(jnp.dot(atom_out, agg_weight, preferred_element_type=jnp.float32)).astype(
        jnp.bfloat16
    )
    rows_here, cols_here = (pair_cond.shape[0], pair_cond.shape[1])
    local_token = atom_token - row_rank * rows_here
    onehot = local_token[None, :] == jnp.arange(rows_here, dtype=jnp.int32)[:, None]
    counts = jnp.sum(onehot.astype(jnp.float32), 1)
    token_sum = jnp.einsum(
        "ta,sad->std", onehot.astype(jnp.bfloat16), hidden, preferred_element_type=jnp.float32
    )
    token_in = token_sum / counts[None, :, None]
    pnorm = layer_norm(pair_cond.astype(jnp.float32)).astype(jnp.bfloat16)
    bias_raw = jnp.dot(pnorm, pair_weight, preferred_element_type=jnp.float32)
    qidx = row_rank * rows_here + jnp.arange(rows_here, dtype=jnp.int32)
    kidx = lax.axis_index("sample") * cols_here + jnp.arange(cols_here, dtype=jnp.int32)
    allowed = (token_mask[None, :] == 1) | (qidx[:, None] == kidx[None, :])
    bias_part = jnp.transpose(
        jnp.where(allowed[:, :, None], bias_raw, -30000.0).astype(jnp.bfloat16), (2, 0, 1)
    )
    bias_rows = lax.all_gather(bias_part, "sample", axis=2, tiled=True)
    tnorm = (layer_norm(token_in) * token_gain).astype(jnp.bfloat16)
    tquery = (
        jnp.dot(tnorm, query_weight, preferred_element_type=jnp.float32)
        .astype(jnp.bfloat16)
        .reshape(samples, rows_here, HEADS, HEAD_DIM)
    )
    gate = jnp.dot(tnorm, gate_weight, preferred_element_type=jnp.float32)
    tscale = 1.0 / HEAD_DIM**0.5
    tkeys = jnp.dot(tnorm, key_weight, preferred_element_type=jnp.float32).astype(jnp.bfloat16)
    tvals = jnp.dot(tnorm, value_weight, preferred_element_type=jnp.float32).astype(jnp.bfloat16)
    attend_tkeys = lax.all_gather(tkeys, "row", axis=1, tiled=True)
    attend_tvals = lax.all_gather(tvals, "row", axis=1, tiled=True)
    running = jnp.full((samples, HEADS, rows_here), -jnp.inf, jnp.float32)
    total = jnp.zeros((samples, HEADS, rows_here), jnp.float32)
    accum = jnp.zeros((samples, HEADS, rows_here, HEAD_DIM), jnp.float32)
    count = attend_tkeys.shape[1]
    attend_tkeys = attend_tkeys.reshape(samples, count, HEADS, HEAD_DIM)
    attend_tvals = attend_tvals.reshape(samples, count, HEADS, HEAD_DIM)
    tbias = bias_rows.astype(jnp.float32)
    scores = (
        jnp.einsum("sqhd,skhd->shqk", tquery, attend_tkeys, preferred_element_type=jnp.float32)
        * tscale
        + tbias[None]
    )
    newmax = jnp.max(scores, -1)
    expd = jnp.exp(scores - newmax[..., None])
    factor = jnp.exp(running - newmax)
    total = total * factor + jnp.sum(expd, -1)
    accum = accum * factor[..., None] + jnp.einsum(
        "shqk,skhd->shqd",
        expd.astype(jnp.bfloat16),
        attend_tvals,
        preferred_element_type=jnp.float32,
    )
    tmix = accum / total[..., None]
    tmix = jnp.transpose(tmix, (0, 2, 1, 3)).reshape(samples, rows_here, HEADS * HEAD_DIM)
    gated = (tmix * jax.nn.sigmoid(gate)).astype(jnp.bfloat16)
    return (token_in + jnp.dot(gated, out_weight, preferred_element_type=jnp.float32)).astype(
        jnp.bfloat16
    )


def solution(mesh):
    placed = (
        P("sample", "row", None),
        P("row"),
        P("row", "sample", None),
        P("sample"),
        P(),
        P(),
        P(),
        P(),
        P(),
        P(),
        P(),
        P(),
        P(),
        P(),
        P(),
        P(),
    )
    return jax.shard_map(
        shards, mesh=mesh, in_specs=placed, out_specs=P("sample", "row", None), check_vma=False
    )
```

profile of v0, /device:TPU:1, one launch (start us, length us, event | category | flops | bytes accessed | tf_op | source)
XLA Modules:
  0.0 217.6 jit_solution(3594098821739291839)
XLA Ops:
  6.5 1.5 convert_reduce_fusion.1
  8.0 1.8 fusion.54
  9.8 1.8 fusion.55
  11.6 4.9 %collective-permute-start = (bf16[2,48,128]{2,1,0:T(8,128)(2,1)S(1)}, bf16[2,48,128]{2,1,0:T(8,128)(2,1)}, u32[]{:S(2)}, u32[]{:S(2)}) collective-permute-start(bf16[2,48,128]{2,1,0:T(8,128)(2,1)S(1)} %get-tuple-element.13), channel_id=1, source_target_pairs={{0,16},{16,32},{32,48},{48,64},{64,80},{80,96},{96,112},{112,128},... | collective-permute-start | bytes 73736 | tf_op jit(solution)/shard_map/ppermute | solution.py:21
  16.6 2.1 collective-permute-start.1
  18.7 0.7 broadcast_compare_fusion
  19.3 0.7 convert_reduce_fusion
  20.0 2.3 %fusion.14 = f32[72,72]{1,0:T(8,128)S(1)} fusion(bf16[72,72,128]{2,1,0:T(8,128)(2,1)S(1)} %copy-done.4, f32[72,72]{1,0:T(8,128)S(1)} %broadcast_multiply_fusion), kind=kLoop, calls=%fused_computation.22 | loop fusion | flops 2649024 | bytes 1368576 | tf_op jit(solution)/shard_map/reduce_sum | solution.py:30
  22.5 2.2 %fusion.61 = bf16[16,72,72]{2,0,1:T(8,128)(2,1)S(1)} fusion(bf16[72,72,128]{2,1,0:T(8,128)(2,1)S(1)} %copy-done.4, f32[72,72]{1,0:T(8,128)S(1)} %add_rsqrt_fusion, f32[72,72]{1,0:T(8,128)S(1)} %broadcast_multiply_fusion, pred[72,72]{1,0:T(8,128)(4,1)S(1)} %compare_or_fusion, bf16[128,16]{0,1:T(8,128)(2,1)S(1)} %copy-done.14), kind=kOutput, calls=%fused_computation.69 | convolution fusion | flops 24053760 | bytes 1543744 | tf_op jit(solution)/shard_map/dot_general | solution.py:106
  24.7 1.1 copy.50
  25.9 0.2 all-gather.4.cloned.1.call-start
  26.1 0.3 convolution_convert_fusion.2
  26.5 0.6 convert_reduce_fusion.2
  27.2 2.1 reshape.158
  29.2 1.1 convolution_convert_fusion.1
  30.3 0.4 fusion.91
  30.7 0.3 pad_maximum_fusion
  31.0 2.5 %copy.44 = bf16[2,36,128,128]{2,3,1,0:T(8,128)(2,1)} copy(bf16[2,36,128,128]{3,2,1,0:T(8,128)(2,1)S(1)} %pad_maximum_fusion) | data formatting | bytes 4718592 | tf_op jit(solution)/shard_map/concatenate | solution.py:64
  33.4 1.4 convolution_convert_fusion
  34.8 0.4 fusion.90
  35.2 0.3 pad_maximum_fusion.1
  35.5 2.5 %copy.46 = bf16[2,36,128,128]{2,3,1,0:T(8,128)(2,1)} copy(bf16[2,36,128,128]{3,2,1,0:T(8,128)(2,1)S(1)} %pad_maximum_fusion.1) | data formatting | bytes 4718592 | tf_op jit(solution)/shard_map/concatenate | solution.py:67
  38.0 3.9 %fusion.9 = (f32[2,36,4,32]{3,2,1,0:T(4,128)S(1)}, f32[2,36,4,32,128]{4,3,2,1,0:T(8,128)S(1)}) fusion(pred[36,128]{1,0:T(8,128)(4,1)S(1)} %fusion.81, bf16[2,36,128,4,32]{2,4,3,1,0:T(8,128)(2,1)} %bitcast.84, bf16[2,36,32,4,32]{4,3,2,1,0:T(4,128)(2,1)} %reshape.158), kind=kOutput, calls=%fused_computation.14 | convolution fusion | flops 79027200 | bytes 7709184 | tf_op jit(solution)/shard_map/swqhd,swkhd->swhqk/dot_general | solution.py:75
  41.9 2.9 %fusion.10 = f32[2,36,4,32]{3,2,1,0:T(4,128)S(1)} fusion(f32[2,36,4,32,128]{4,3,2,1,0:T(8,128)S(1)} %get-tuple-element.16, f32[2,36,4,32]{3,2,1,0:T(4,128)S(1)} %get-tuple-element.15, pred[36,128]{1,0:T(8,128)(4,1)S(1)} %fusion.81), kind=kLoop, calls=%fused_computation.15 | loop fusion | flops 4709376 | bytes 4796928 | tf_op jit(solution)/shard_map/reduce_sum | solution.py:80
  44.8 3.2 %fusion.8 = bf16[2,36,32,4,32]{4,2,3,1,0:T(8,128)(2,1)S(1)} fusion(f32[2,36,32,4]{2,3,1,0:T(4,128)S(1)} %bitcast.90, bf16[2,36,128,4,32]{2,4,3,1,0:T(8,128)(2,1)S(1)} %bitcast.88, f32[2,36,4,32,128]{4,3,2,1,0:T(8,128)S(1)} %get-tuple-element.16, f32[2,36,4,32]{3,2,1,0:T(4,128)S(1)} %get-tuple-element.15, pred[36,128]{1,0:T(8,128)(4,1)S(1)} %fusion.81), kind=kOutput, calls=%fused_computation.11 | convolution fusion | flops 80805888 | bytes 7746048 | tf_op jit(solution)/shard_map/swhqk,swkhd->swhqd/dot_general | solution.py:82
  48.0 2.7 %copy.47 = bf16[2,36,32,4,32]{4,3,2,1,0:T(4,128)(2,1)} copy(bf16[2,36,32,4,32]{4,2,3,1,0:T(8,128)(2,1)S(1)} %fusion.8) | data formatting | bytes 1179648 | tf_op jit(solution)/shard_map/convert_element_type | solution.py:90
  50.7 3.3 %convert_element_type.79 = bf16[2,1152,128]{2,1,0:T(8,128)(2,1)S(1)} reshape(bf16[2,36,32,4,32]{4,3,2,1,0:T(4,128)(2,1)} %copy.47) | data formatting | bytes 1179648 | tf_op jit(solution)/shard_map/convert_element_type | solution.py:90
  54.1 0.3 fusion.16
  54.4 3.3 %fusion.93 = (f32[2,72]{1,0:T(2,128)S(1)}, f32[2,72,768]{2,1,0:T(8,128)S(1)}) fusion(f32[72]{0:T(128)S(1)} %copy-done.12, s32[1152]{0:T(1024)S(1)} %broadcast_subtract_fusion, bf16[2,1152,128]{2,1,0:T(8,128)(2,1)S(1)} %fusion.16, bf16[128,768]{1,0:T(8,128)(2,1)} %param.24), kind=kOutput, calls=%fused_computation.113 | convolution fusion | flops 711631744 | bytes 1234272 | tf_op jit(solution)/shard_map/ta,sad->std/dot_general | solution.py:101
  57.7 0.2 multiply_reduce_fusion
  58.0 1.1 convolution_convert_fusion.4
  59.1 0.3 all-gather.8.cloned.1.call-start
  59.4 1.1 convolution_convert_fusion.3
  60.5 1.7 convolution_convert_fusion.5
  62.2 0.2 copy.48
  62.4 49.5 %all-gather.6.cloned.1.call-done = bf16[16,72,1152]{1,0,2:T(8,128)(2,1)} async-done(((bf16[16,72,72]{1,0,2:T(8,128)(2,1)}), bf16[16,72,1152]{1,0,2:T(8,128)(2,1)}) %all-gather.6.cloned.1.call-update) | async-done | bytes 2654224 | tf_op jit(solution)/shard_map/all_gather | solution.py:113
  111.9 6.6 %copy.51 = bf16[16,72,1152]{2,1,0:T(8,128)(2,1)} copy(bf16[16,72,1152]{1,0,2:T(8,128)(2,1)} %all-gather.6.cloned.1.call-done) | data formatting | bytes 5308416 | tf_op jit(solution)/shard_map/all_gather | solution.py:113
  118.5 4.5 %convert_element_type.90 = f32[16,72,1152]{2,1,0:T(8,128)} convert(bf16[16,72,1152]{2,1,0:T(8,128)(2,1)} %copy.51) | non-fusion elementwise | flops 1327104 | bytes 7962624 | tf_op jit(solution)/shard_map/convert_element_type | solution.py:132
  123.0 28.5 %all-gather.4.cloned.1.call-done = bf16[2,1152,768]{2,1,0:T(8,128)(2,1)} async-done(((bf16[2,72,768]{2,1,0:T(8,128)(2,1)}), bf16[2,1152,768]{2,1,0:T(8,128)(2,1)}) %all-gather.4.cloned.1.call-update) | async-done | bytes 3538960 | tf_op jit(solution)/shard_map/all_gather | solution.py:124
  151.5 5.8 %copy.49 = bf16[2,1152,768]{1,2,0:T(8,128)(2,1)} copy(bf16[2,1152,768]{2,1,0:T(8,128)(2,1)} %all-gather.4.cloned.1.call-done) | data formatting | bytes 7077888 | tf_op jit(solution)/shard_map/all_gather | solution.py:124
  157.3 5.5 %fusion = (f32[2,16,72]{2,1,0:T(8,128)S(1)}, f32[2,16,72,1152]{3,2,1,0:T(8,128)S(1)}) fusion(f32[16,72,1152]{2,1,0:T(8,128)} %convert_element_type.90, bf16[2,72,16,48]{1,3,2,0:T(8,128)(2,1)S(1)} %bitcast.89, bf16[2,1152,16,48]{1,3,2,0:T(8,128)(2,1)} %bitcast.83), kind=kOutput, calls=%fused_computation.2 | convolution fusion | flops 262764288 | bytes 19694592 | tf_op jit(solution)/shard_map/sqhd,skhd->shqk/dot_general | solution.py:134
  162.8 2.7 %fusion.1 = f32[2,16,72]{2,1,0:T(8,128)S(1)} fusion(f32[2,16,72,1152]{3,2,1,0:T(8,128)S(1)} %get-tuple-element.20, f32[2,16,72]{2,1,0:T(8,128)S(1)} %get-tuple-element.19, f32[16,72,1152]{2,1,0:T(8,128)S(1)} %bitcast.81), kind=kLoop, calls=%fused_computation.3 | loop fusion | flops 10614528 | bytes 15943680 | tf_op jit(solution)/shard_map/reduce_sum | solution.py:141
  165.5 1.3 copy-done.2
  166.8 25.5 %all-gather.8.cloned.1.call-done = bf16[2,1152,768]{2,1,0:T(8,128)(2,1)} async-done(((bf16[2,72,768]{2,1,0:T(8,128)(2,1)}), bf16[2,1152,768]{2,1,0:T(8,128)(2,1)}) %all-gather.8.cloned.1.call-update) | async-done | bytes 3538960 | tf_op jit(solution)/shard_map/all_gather | solution.py:125
  192.3 5.8 %copy.52 = bf16[2,1152,768]{1,2,0:T(8,128)(2,1)} copy(bf16[2,1152,768]{2,1,0:T(8,128)(2,1)} %all-gather.8.cloned.1.call-done) | data formatting | bytes 7077888 | tf_op jit(solution)/shard_map/all_gather | solution.py:125
  198.1 9.5 %fusion.66 = f32[2,72,16,48]{1,3,2,0:T(8,128)S(1)} fusion(bf16[2,1152,16,48]{1,3,2,0:T(8,128)(2,1)} %bitcast.82, f32[2,16,72,1152]{3,2,1,0:T(8,128)} %copy-done.2, f32[2,16,72]{2,1,0:T(8,128)S(1)} %get-tuple-element.19, f32[16,72,1152]{2,1,0:T(8,128)} %convert_element_type.90, f32[2,72,16]{1,2,0:T(8,128)S(1)} %bitcast_add_fusion, ...), kind=kOutput, calls=%fused_computation.70 | convolution fusion | flops 265641984 | bytes 19934208 | tf_op jit(solution)/shard_map/shqk,skhd->shqd/dot_general | solution.py:142
  207.7 0.2 copy.53
  207.9 3.1 %fusion.52 = bf16[2,72,768]{2,1,0:T(8,128)(2,1)} fusion(f32[2,72,768]{2,1,0:T(8,128)S(1)} %get-tuple-element.18, bf16[768,768]{1,0:T(8,128)(2,1)} %param.31, f32[2,72,768]{2,1,0:T(8,128)S(1)} %copy.53, bf16[768,768]{1,0:T(8,128)(2,1)} %param.30, f32[768]{0:T(1024)S(1)} %copy-done.8, f32[2,72]{1,0:T(2,128)S(1)} %add_rsqrt_fusion.2, ...), kind=kOutput, calls=%fused_computation.57 | convolution fusion | flops 340955136 | bytes 3469440 | tf_op jit(solution)/shard_map/dot_general | solution.py:151
  (54 shorter events, 0.4 us)
Async XLA Ops:
  6.5 51.4 %copy-start = (bf16[768,768]{1,0:T(8,128)(2,1)S(1)}, bf16[768,768]{1,0:T(8,128)(2,1)}, u32[]{:S(2)}) copy-start(bf16[768,768]{1,0:T(8,128)(2,1)} %param.28) | copy-start | bytes 3538948
  6.5 12.8 %copy-start.4 = (bf16[72,72,128]{2,1,0:T(8,128)(2,1)S(1)}, bf16[72,72,128]{2,1,0:T(8,128)(2,1)}, u32[]{:S(2)}) copy-start(bf16[72,72,128]{2,1,0:T(8,128)(2,1)} %param.18) | copy-start | bytes 3981316
  6.5 15.9 %copy-start.14 = (bf16[128,16]{0,1:T(8,128)(2,1)S(1)}, bf16[128,16]{0,1:T(8,128)(2,1)}, u32[]{:S(2)}) copy-start(bf16[128,16]{0,1:T(8,128)(2,1)} %param.25) | copy-start | bytes 12292
  6.5 105.3 %all-gather.6.cloned.1.call-start = ((), (), s32[]{:S(2)}) async-start(), calls=%async_computation.1 | async-start | bytes 5013504 | tf_op jit(solution)/shard_map/all_gather | solution.py:113
  11.6 17.7 %copy-start.5 = (bf16[2,1152,128]{2,1,0:T(8,128)(2,1)}, bf16[2,1152,128]{2,1,0:T(8,128)(2,1)S(1)}, u32[]{:S(2)}) copy-start(bf16[2,1152,128]{2,1,0:T(8,128)(2,1)S(1)} %fusion.55) | copy-start | bytes 1769476
  11.6 17.6 %collective-permute-start = (bf16[2,48,128]{2,1,0:T(8,128)(2,1)S(1)}, bf16[2,48,128]{2,1,0:T(8,128)(2,1)}, u32[]{:S(2)}, u32[]{:S(2)}) collective-permute-start(bf16[2,48,128]{2,1,0:T(8,128)(2,1)S(1)} %get-tuple-element.13), channel_id=1, source_target_pairs={{0,16},{16,32},{32,48},{48,64},{64,80},{80,96},{96,112},{112,128},... | collective-permute-start | bytes 73736 | tf_op jit(solution)/shard_map/ppermute | solution.py:21
  16.6 12.7 %collective-permute-start.1 = (bf16[2,48,128]{2,1,0:T(8,128)(2,1)S(1)}, bf16[2,48,128]{2,1,0:T(8,128)(2,1)}, u32[]{:S(2)}, u32[]{:S(2)}) collective-permute-start(bf16[2,48,128]{2,1,0:T(8,128)(2,1)S(1)} %get-tuple-element.14), channel_id=1, source_target_pairs={{16,0},{32,16},{48,32},{64,48},{80,64},{96,80},{112,96},{128,112},... | collective-permute-start | bytes 73736 | tf_op jit(solution)/shard_map/ppermute | solution.py:22
  20.0 6.1 %copy-start.10 = (bf16[128,128]{1,0:T(8,128)(2,1)S(1)}, bf16[128,128]{1,0:T(8,128)(2,1)}, u32[]{:S(2)}) copy-start(bf16[128,128]{1,0:T(8,128)(2,1)} %param.20) | copy-start | bytes 98308
  22.3 4.1 %copy-start.11 = (s32[1152]{0:T(1024)S(1)}, s32[1152]{0:T(1024)}, u32[]{:S(2)}) copy-start(s32[1152]{0:T(1024)} %param.17) | copy-start | bytes 13828
  24.7 4.5 %copy-start.13 = (bf16[128,128]{1,0:T(8,128)(2,1)S(1)}, bf16[128,128]{1,0:T(8,128)(2,1)}, u32[]{:S(2)}) copy-start(bf16[128,128]{1,0:T(8,128)(2,1)} %param.21) | copy-start | bytes 98308
  25.9 125.6 %all-gather.4.cloned.1.call-start = ((), (), s32[]{:S(2)}) async-start(), calls=%async_computation | async-start | bytes 3760128 | tf_op jit(solution)/shard_map/all_gather | solution.py:124
  41.9 2.9 %copy-start.6 = (bf16[2,36,128,128]{2,3,1,0:T(8,128)(2,1)S(1)}, bf16[2,36,128,128]{2,3,1,0:T(8,128)(2,1)}, u32[]{:S(2)}) copy-start(bf16[2,36,128,128]{2,3,1,0:T(8,128)(2,1)} %copy.46) | copy-start | bytes 7077892
  48.0 6.0 %copy-start.3 = (bf16[2,1152,128]{2,1,0:T(8,128)(2,1)S(1)}, bf16[2,1152,128]{2,1,0:T(8,128)(2,1)}, u32[]{:S(2)}) copy-start(bf16[2,1152,128]{2,1,0:T(8,128)(2,1)} %param.16) | copy-start | bytes 1769476
  48.0 6.0 %copy-start.9 = (bf16[128,128]{1,0:T(8,128)(2,1)S(1)}, bf16[128,128]{1,0:T(8,128)(2,1)}, u32[]{:S(2)}) copy-start(bf16[128,128]{1,0:T(8,128)(2,1)} %param.23) | copy-start | bytes 98308
  50.7 3.7 %copy-start.12 = (f32[72]{0:T(128)S(1)}, f32[72]{0:T(128)}, u32[]{:S(2)}) copy-start(f32[72]{0:T(128)} %convert_reduce_fusion.2) | copy-start | bytes 868
  54.4 3.6 %copy-start.8 = (f32[768]{0:T(1024)S(1)}, f32[768]{0:T(1024)}, u32[]{:S(2)}) copy-start(f32[768]{0:T(1024)} %param.26) | copy-start | bytes 9220
  54.4 5.0 %copy-start.7 = (bf16[768,768]{1,0:T(8,128)(2,1)S(1)}, bf16[768,768]{1,0:T(8,128)(2,1)}, u32[]{:S(2)}) copy-start(bf16[768,768]{1,0:T(8,128)(2,1)} %param.29) | copy-start | bytes 3538948
  59.1 133.2 %all-gather.8.cloned.1.call-start = ((), (), s32[]{:S(2)}) async-start(), calls=%async_computation.2 | async-start | bytes 3760128 | tf_op jit(solution)/shard_map/all_gather | solution.py:125
  157.2 5.6 %slice-start = ((s8[5308416]{0:T(1024)(128)(4,1)}), s8[4194304]{0:T(1024)(128)(4,1)S(1)}, s32[]{:S(2)}) async-start(s8[5308416]{0:T(1024)(128)(4,1)} %bitcast.80), calls=%async_computation.3 | async-start | bytes 8388608
  157.3 5.6 %slice-start.1 = ((s8[5308416]{0:T(1024)(128)(4,1)}), s8[1114112]{0:T(1024)(128)(4,1)S(1)}, s32[]{:S(2)}) async-start(s8[5308416]{0:T(1024)(128)(4,1)} %bitcast.80), calls=%async_computation.4 | async-start | bytes 2228224
  162.8 4.0 %copy-start.2 = (f32[2,16,72,1152]{3,2,1,0:T(8,128)}, f32[2,16,72,1152]{3,2,1,0:T(8,128)S(1)}, u32[]{:S(2)}) copy-start(f32[2,16,72,1152]{3,2,1,0:T(8,128)S(1)} %get-tuple-element.20) | copy-start | bytes 31850500
  207.7 3.4 %copy-start.1 = (bf16[768,768]{1,0:T(8,128)(2,1)S(1)}, bf16[768,768]{1,0:T(8,128)(2,1)}, u32[]{:S(2)}) copy-start(bf16[768,768]{1,0:T(8,128)(2,1)} %param.28) | copy-start | bytes 3538948
Sparse Core Ops, SparseCore 0:
  26.0 85.8 all-gather.5
  113.7 37.7 all-gather.3
  153.3 38.9 all-gather.7
where the time goes:
time: 218 us
  waiting for transfers between devices  104 us (48%)
  matrix products  37.7 us (17%)
  local copies, waits for them, and re-layouts  34.8 us (16%)
  other arithmetic  20.3 us (9%)
  between operations  13.6 us (6%)
  starting transfers between devices  7.52 us (3%)
    all_gather x1, waiting for transfers between devices, shards(): bias_rows = lax.all_gather(bias_part, 'sample', axis=2, tiled=True)  49.5 us
    all_gather x1, waiting for transfers between devices, shards(): attend_tkeys = lax.all_gather(tkeys, 'row', axis=1, tiled=True)  28.5 us
    all_gather x1, waiting for transfers between devices, shards(): attend_tvals = lax.all_gather(tvals, 'row', axis=1, tiled=True)  25.5 us
    dot_general x1, matrix products, shards(): jnp.einsum('shqk,skhd->shqd', expd.astype(jnp.bfloat16), attend_tvals, pr...  9.51 us
    all_gather x1, local copies, waits for them, and re-layouts, shards(): bias_rows = lax.all_gather(bias_part, 'sample', axis=2, tiled=True)  6.6 us
    convert_element_type x2, local copies, waits for them, and re-layouts, shards(): jnp.transpose(amix, (0, 1, 3, 2, 4)).reshape(samples, atoms, chans)  6 us
    all_gather x1, local copies, waits for them, and re-layouts, shards(): attend_tvals = lax.all_gather(tvals, 'row', axis=1, tiled=True)  5.82 us
    all_gather x1, local copies, waits for them, and re-layouts, shards(): attend_tkeys = lax.all_gather(tkeys, 'row', axis=1, tiled=True)  5.78 us
  transfers between devices with their start and end apart: 5, of which 3 were waited for; matrix products, arithmetic and copies ran while one was open for 31% of the time, Pallas kernels for 0%

commit v1 on v0

v1 whole, which is shorter than its diff:
```python
import jax
import jax.numpy as jnp
from jax import lax
from jax.experimental import pallas as pl
from jax.experimental.pallas import tpu as pltpu
from jax.sharding import PartitionSpec as P

HEADS = 16
HEAD_DIM = 48
AHEADS = 4
AHEAD_DIM = 32
QWIN = 32
KWIN = 128
RIM = 48
TOK = 72
PAD = 80
ATOMS = 1152
CA = 128
D = 768
LANES = HEADS * TOK
F32 = jnp.float32
BF16 = jnp.bfloat16
NEG = -1e30
CHUNKS = ((0, 256, 0, 256), (256, 256, 128, 256), (512, 256, 256, 384), (768, 256, 384, 384), (1024, 128, 640, 128))


def dot(a, b):
    return jnp.dot(a, b, preferred_element_type=F32)


def dot_nt(a, b):
    return lax.dot_general(a, b, (((1,), (1,)), ((), ())), preferred_element_type=F32)


def layer_norm(x):
    mean = jnp.mean(x, -1, keepdims=True)
    centre = x - mean
    var = jnp.mean(centre * centre, -1, keepdims=True)
    return centre * lax.rsqrt(var + 1e-05)


def iota(shape, dim):
    return lax.broadcasted_iota(jnp.int32, shape, dim)


MESH = pl.DeviceIdType.MESH
KEYS = 16 * PAD
HALF = 8 * PAD
PARTS = ((0, 48), (48, 32))


def pair_part(pair_ref, mask_ref, weight_ref, table_ref, out, row, col, unroll=12):
    weight_t = weight_ref[...]

    def step(g, carry):
        normed = [layer_norm(pair_ref[g * unroll + u].astype(F32)).astype(BF16) for u in range(unroll)]
        raw = [dot_nt(weight_t, n) for n in normed]
        for u in range(unroll):
            table_ref[pl.ds(g * unroll + u, HEADS, stride=TOK), :TOK] = raw[u]
        return carry

    lax.fori_loop(0, TOK // unroll, step, 0)
    kidx = col * TOK + iota((TOK, TOK), 1)
    qidx = row * TOK + iota((TOK, TOK), 0)
    allowed = (mask_ref[...] == 1) | (qidx == kidx)
    for h in range(HEADS):
        rows = pl.ds(h * TOK, TOK)
        table_ref[rows, :TOK] = jnp.where(allowed, table_ref[rows, :TOK], -30000.0)
    for n in range(LANES // 128):
        part = table_ref[n * 128 : (n + 1) * 128, :].T[:TOK]
        filled = jnp.concatenate([part, jnp.full((PAD - TOK, 128), NEG, F32)], axis=0)
        out[:, n * 128 : (n + 1) * 128] = filled.astype(BF16)


def atom_project(s, halo_ref, feat_ref, wq, wk, wv, normed_ref, q_ref, k_ref, v_ref, row, rows):
    def norm_step(start, source):
        normed_ref[pl.ds(start, source.shape[0]), :] = layer_norm(source.astype(F32)).astype(BF16)

    norm_step(0, halo_ref[0, s])
    norm_step(RIM + ATOMS, halo_ref[1, s])
    for c in range(9):
        norm_step(RIM + c * 128, feat_ref[s, c * 128 : (c + 1) * 128])
    for c in range(3):
        here = pl.ds(c * 416, 416)
        block = normed_ref[here, :]
        k_ref[here, :] = dot(block, wk).astype(BF16)
        v_ref[here, :CA] = dot(block, wv).astype(BF16)
        v_ref[here, CA:] = jnp.ones((416, CA), BF16)
        q_ref[pl.ds(c * 384, 384), :] = dot(normed_ref[pl.ds(RIM + c * 384, 384), :], wq).astype(BF16)
    last = RIM + ATOMS
    first_key = k_ref[RIM : RIM + 16, :].astype(F32)[:1]
    last_key = k_ref[last - 16 : last, :].astype(F32)[15:]
    for outside, start, key in ((row == 0, 0, first_key), (row == rows - 1, last, last_key)):
        here = pl.ds(start, RIM)
        k_ref[here, :] = jnp.where(outside, jnp.broadcast_to(key, (RIM, CA)), k_ref[here, :].astype(F32)).astype(BF16)
        v_ref[here, :] = jnp.where(outside, 0.0, v_ref[here, :].astype(F32)).astype(BF16)


def atom_windows(q_ref, k_ref, v_ref, att_ref, first, group=12):
    head_of = iota((AHEADS * QWIN, CA), 0) // QWIN == iota((AHEADS * QWIN, CA), 1) // AHEAD_DIM
    lane_head = iota((QWIN, CA), 1) // AHEAD_DIM
    factor = 1.4426950408889634 / AHEAD_DIM**0.5
    starts = [pl.multiple_of(first + u * QWIN, QWIN) for u in range(group)]
    scores = []
    for start in starts:
        q = q_ref[pl.ds(start, QWIN), :]
        stacked = jnp.where(head_of, jnp.concatenate([q] * AHEADS, axis=0), jnp.zeros((), BF16))
        scores.append(dot_nt(stacked, k_ref[pl.ds(start, KWIN), :]))
    exps = [jnp.exp2((sc - jnp.max(sc, -1, keepdims=True)) * factor).astype(BF16) for sc in scores]
    for start, e in zip(starts, exps):
        both = dot(e, v_ref[pl.ds(start, KWIN), :])
        top, low = both[:QWIN, :CA], both[:QWIN, CA:]
        for h in range(1, AHEADS):
            here = slice(h * QWIN, (h + 1) * QWIN)
            top = jnp.where(lane_head == h, both[here, :CA], top)
            low = jnp.where(lane_head == h, both[here, CA:], low)
        att_ref[pl.ds(start, QWIN), :] = (top / low).astype(BF16)


def atom_tokens(s, feat_ref, token_ref, wo, agg_ref, gain_ref, att_ref, token_in_ref, row):
    total = jnp.zeros((TOK, D), F32)
    counts = jnp.zeros((TOK, 1), F32)
    for c in range(3):
        here = pl.ds(c * 384, 384)
        out = (feat_ref[s, here, :].astype(F32) + dot(att_ref[here, :], wo)).astype(BF16)
        hidden = jnp.maximum(dot(out, agg_ref[...]), 0.0).astype(BF16)
        onehot = token_ref[:, c * 384 : (c + 1) * 384] - row * TOK == iota((TOK, 384), 0)
        total += dot(onehot.astype(BF16), hidden)
        counts += jnp.sum(onehot.astype(F32), -1, keepdims=True)
    token_in = total / counts
    token_in_ref[s] = token_in
    tnorm = layer_norm(token_in) * gain_ref[...]
    return jnp.concatenate([tnorm, jnp.zeros((PAD - TOK, D), F32)], axis=0).astype(BF16)


def query_prep(qt_ref, slab, chunk):
    lo, width, clo, cwidth = chunk
    lane = lo + iota((TOK, width), 1)
    fold = (lane % TOK == iota((TOK, width), 0)).astype(BF16)
    own_head = (lo + iota((cwidth, width), 1)) // TOK == (clo + iota((cwidth, width), 0)) // HEAD_DIM
    query = jnp.where(own_head, dot(qt_ref[slab, pl.ds(clo, cwidth), :], fold), 0.0).astype(BF16)
    return fold, own_head, query


def attend(k_ref, vt_ref, bias_of, qt_ref, scores_ref, p_ref, mix_ref, after_slab, blk=PAD * 2):
    mix_ref[...] = jnp.zeros_like(mix_ref)
    work = [(slab, chunk) for slab in range(2) for chunk in CHUNKS]
    blocks = KEYS // blk
    state = {}
    for i in range(len(work) + 2):
        now = work[i] if i < len(work) else None
        exps = work[i - 1] if 0 <= i - 1 < len(work) else None
        vals = work[i - 2] if i >= 2 else None
        if exps:
            top = jnp.max(state[i - 1][3], axis=0, keepdims=True)
            total = jnp.zeros((8, exps[1][1]), F32)
        if now:
            lo, width, clo, cwidth = now[1]
            state[i] = list(query_prep(qt_ref, *now)) + [jnp.full((8, width), -3e38, F32)]
            ahead = dot(k_ref[0:blk, clo : clo + cwidth], state[i][2])
        if vals:
            _, vwidth, vlo, vcwidth = vals[1]
            out = dot(vt_ref[pl.ds(vlo, vcwidth), :], p_ref[i % 2, :, :vwidth])
        for b in range(blocks):
            here = pl.ds(b * blk, blk)
            if now:
                raw = ahead
                if b + 1 < blocks:
                    ahead = dot(k_ref[(b + 1) * blk : (b + 2) * blk, clo : clo + cwidth], state[i][2])
            if exps:
                ewidth = exps[1][1]
                e = jnp.exp(scores_ref[(i - 1) % 2, here, :ewidth] - top)
                total += jnp.sum(e.reshape(blk // 8, 8, ewidth), axis=0)
                p_ref[(i - 1) % 2, here, :ewidth] = e.astype(BF16)
            if now:
                sc = raw * (1.0 / HEAD_DIM**0.5) + bias_of(now[0], b, blk, lo, width)
                scores_ref[i % 2, here, :width] = sc
                state[i][3] = jnp.maximum(state[i][3], jnp.max(sc.reshape(blk // 8, 8, width), axis=0))
        if exps:
            state[i - 1].append(jnp.sum(total, axis=0, keepdims=True))
        if vals:
            fold, own_head, _, _, vsum = state.pop(i - 2)
            out = jnp.where(own_head, out * (1.0 / vsum), 0.0)
            high = out.astype(BF16)
            rest = (out - high.astype(F32)).astype(BF16)
            mix_ref[vals[0], :, vlo : vlo + vcwidth] += dot_nt(fold, high) + dot_nt(fold, rest)
            if vals[1] is CHUNKS[-1]:
                after_slab(vals[0])


def whole_kernel(pair_ref, mask_ref, pair_w_ref, feat_ref, token_ref, wq, wk, wv, wo, agg_ref, gain_ref,
                 query_hbm, key_hbm, value_hbm, gate_hbm, out_hbm, out_ref,
                 table_ref, halo_ref, normed_ref, q_ref, k_ref, v_ref, att_ref, token_in_ref, give_ref, tall_ref, bias_ref,
                 weights_ref, wvt_ref, keys_ref, vt_ref, qt_ref, sig_ref, scores_ref, p_ref, mix_ref, back_send, back_recv,
                 load_sem, halo_send, halo_recv, bias_send, bias_recv, twin_send, twin_recv, tok_send, tok_recv,
                 pass_send, pass_recv):
    row, col = lax.axis_index("row"), lax.axis_index("sample")
    rows, cols = lax.axis_size("row"), lax.axis_size("sample")
    core, zl, y = row % 2, (row // 2) % 2, row // 4
    x, zh = col % 4, col // 4
    twin, zpair = row + 1 - 2 * core, row + 2 - 4 * zl
    y_up, y_down = (row + 4) % rows, (row + rows - 4) % rows
    r_up, r_down = (row + 1) % rows, (row + rows - 1) % rows
    x_up, x_down = zh * 4 + (x + 1) % 4, zh * 4 + (x + 3) % 4
    z_up, z_down = (col + 4) % cols, (col + cols - 4) % cols
    loads = []
    for n, source in enumerate((query_hbm, key_hbm, value_hbm, gate_hbm, out_hbm)):
        loads.append(pltpu.make_async_copy(source, weights_ref.at[n], load_sem.at[n]))
        loads[-1].start()

    barrier = pltpu.get_barrier_semaphore()
    for peer in (twin, zpair, y_up, y_down, r_up, r_down):
        pl.semaphore_signal(barrier, inc=1, device_id=(peer, col), device_id_type=MESH)
    for peer in (x_up, x_down, z_up, z_down):
        pl.semaphore_signal(barrier, inc=1, device_id=(row, peer), device_id_type=MESH)
    pl.semaphore_wait(barrier, 10)

    sent = []

    def send(src, dst, send_sem, recv_sem, peer_row, peer_col):
        copy = pltpu.make_async_remote_copy(src_ref=src, dst_ref=dst, send_sem=send_sem, recv_sem=recv_sem,
                                            device_id=(peer_row, peer_col), device_id_type=MESH)
        copy.start()
        sent.append(copy)

    def wait(dst, send_sem, recv_sem, peer_row, peer_col):
        pltpu.make_async_remote_copy(src_ref=dst, dst_ref=dst, send_sem=send_sem, recv_sem=recv_sem,
                                     device_id=(peer_row, peer_col), device_id_type=MESH).wait_recv()

    send(feat_ref.at[:, ATOMS - RIM :], halo_ref.at[0], halo_send.at[0], halo_recv.at[0], r_up, col)
    send(feat_ref.at[:, :RIM], halo_ref.at[1], halo_send.at[1], halo_recv.at[1], r_down, col)

    def bias_slot(zb, xb, part=None):
        at = bias_ref.at[core, xb % 2, zb * 2 + xb // 2]
        return at if part is None else at.at[pl.ds(*part)]

    def bias_wait(role, zb, xb, part=None):
        wait(bias_slot(zb, xb, part), bias_send.at[role], bias_recv.at[role], row, col)

    def bias_give(role, zb, xb, peer, part=None):
        at = bias_slot(zb, xb, part)
        send(at, at, bias_send.at[role], bias_recv.at[role], row, peer)

    z_order = (zh, (zh + 3) % 4, (zh + 1) % 4, (zh + 2) % 4)

    def bias_z_own():
        bias_give(0, zh, x, z_up)
        bias_give(1, zh, x, z_down)

    def bias_z_pass():
        bias_wait(0, z_order[1], x)
        bias_give(2, z_order[1], x, z_up, PARTS[0])
        bias_wait(1, z_order[2], x)
        bias_give(3, z_order[2], x, z_down, PARTS[1])

    def bias_z_end():
        bias_wait(2, z_order[3], x, PARTS[0])
        bias_wait(3, z_order[3], x, PARTS[1])

    def bias_x_own(j):
        bias_give(4 + 4 * j, z_order[j], x, x_up)
        bias_give(5 + 4 * j, z_order[j], x, x_down)

    def bias_x_pass(j):
        bias_wait(4 + 4 * j, z_order[j], (x + 3) % 4)
        bias_give(6 + 4 * j, z_order[j], (x + 3) % 4, x_up, PARTS[0])
        bias_wait(5 + 4 * j, z_order[j], (x + 1) % 4)
        bias_give(7 + 4 * j, z_order[j], (x + 1) % 4, x_down, PARTS[1])

    def bias_x_end(j):
        bias_wait(6 + 4 * j, z_order[j], (x + 2) % 4, PARTS[0])
        bias_wait(7 + 4 * j, z_order[j], (x + 2) % 4, PARTS[1])
        at = bias_ref.at[core, :, pl.ds(z_order[j] * 2, 2)]
        send(at, at, twin_send.at[j], twin_recv.at[j], twin, col)

    def bias_end():
        for j in range(4):
            wait(bias_ref.at[1 - core, :, pl.ds(z_order[j] * 2, 2)], twin_send.at[j], twin_recv.at[j], twin, col)

    def tok_slot(late, yb, zb, part=None):
        at = tall_ref.at[core if late else 1 - core, yb * 2 + zb]
        return at if part is None else at.at[pl.ds(*part)]

    def tok_wait(late, role, yb, zb, part=None):
        n = late * 9 + role
        wait(tok_slot(late, yb, zb, part), tok_send.at[n], tok_recv.at[n], row, col)

    def tok_give(late, role, yb, zb, peer, part=None):
        at, n = tok_slot(late, yb, zb, part), late * 9 + role
        send(at, at, tok_send.at[n], tok_recv.at[n], peer, col)

    zs = (zl, 1 - zl)

    def tok_own(late):
        tok_give(late, 0, y, zl, zpair)
        tok_give(late, 1, y, zl, y_up)
        tok_give(late, 2, y, zl, y_down)

    def tok_second(late):
        tok_wait(late, 0, y, 1 - zl)
        tok_give(late, 5, y, 1 - zl, y_up)
        tok_give(late, 6, y, 1 - zl, y_down)

    def tok_pass(late, j):
        tok_wait(late, 1 + 4 * j, (y + 3) % 4, zs[j])
        tok_give(late, 3 + 4 * j, (y + 3) % 4, zs[j], y_up, PARTS[0])
        tok_wait(late, 2 + 4 * j, (y + 1) % 4, zs[j])
        tok_give(late, 4 + 4 * j, (y + 1) % 4, zs[j], y_down, PARTS[1])

    def tok_end(late):
        for j in range(2):
            tok_wait(late, 3 + 4 * j, (y + 2) % 4, zs[j], PARTS[0])
            tok_wait(late, 4 + 4 * j, (y + 2) % 4, zs[j], PARTS[1])

    pair_part(pair_ref, mask_ref, pair_w_ref, table_ref, bias_slot(zh, x), row, col)
    bias_z_own()
    bias_x_own(0)

    def windows(g):
        atom_windows(q_ref, k_ref, v_ref, att_ref, g * 12 * QWIN)

    def project(s):
        atom_project(s, halo_ref, feat_ref, wq[...], wk[...], wv[...], normed_ref, q_ref, k_ref, v_ref, row, rows)

    def tokens(s):
        return atom_tokens(s, feat_ref, token_ref, wo[...], agg_ref, gain_ref, att_ref, token_in_ref, row)

    wait(halo_ref.at[0], halo_send.at[0], halo_recv.at[0], r_up, col)
    wait(halo_ref.at[1], halo_send.at[1], halo_recv.at[1], r_down, col)
    project(1 - core)
    lax.fori_loop(0, 3, lambda g, c: (windows(g), c)[1], 0)
    give_ref[...] = tokens(1 - core)
    send(give_ref, tall_ref.at[core, y * 2 + zl], pass_send.at[0], pass_recv.at[0], twin, col)
    bias_x_pass(0)
    project(core)
    wait(tall_ref.at[1 - core, y * 2 + zl], pass_send.at[0], pass_recv.at[0], twin, col)
    tok_own(0)
    bias_z_pass()
    bias_x_own(1)
    bias_x_own(2)
    lax.fori_loop(0, 3, lambda g, c: (windows(g), c)[1], 0)
    tok_second(0)
    tok_pass(0, 0)
    bias_x_end(0)
    tall_ref[core, y * 2 + zl] = tokens(core)
    tok_own(1)
    tok_pass(0, 1)
    bias_z_end()
    bias_x_own(3)
    bias_x_pass(1)

    for load in loads:
        load.wait()
    wvt_ref[...] = weights_ref[2].astype(F32).T.astype(BF16)
    tok_second(1)
    tok_pass(1, 0)
    bias_x_pass(2)
    bias_x_end(1)
    for slab in range(2):
        block = tall_ref[core if slab else 1 - core, y * 2 + zl]
        qt_ref[slab] = dot(block, weights_ref[0])[:TOK].T.astype(BF16)
        sig_ref[slab] = jax.nn.sigmoid(dot(block, weights_ref[3])[:TOK])

    def project_tokens(which):
        base = pl.multiple_of(which * HALF, HALF)
        block = tall_ref[which].reshape(HALF, D)
        keys_ref[pl.ds(base, HALF), :] = dot(block, weights_ref[1]).astype(BF16)
        vt_ref[:, pl.ds(base, HALF)] = dot_nt(wvt_ref[...], block).astype(BF16)

    tok_end(0)
    project_tokens(1 - core)
    tok_pass(1, 1)
    bias_x_pass(3)
    bias_x_end(2)
    tok_end(1)
    project_tokens(core)
    bias_x_end(3)
    bias_end()

    def bias_of(slab, b, blk, lo, width):
        per = blk // PAD
        first = b * per
        at = bias_ref[core if slab else 1 - core, first // 8, first % 8 : first % 8 + per, :, lo : lo + width]
        return at.astype(F32).reshape(blk, width)

    def after_slab(slab):
        gated = mix_ref[slab] * sig_ref[slab]
        if slab == 0:
            back_send[...] = jnp.concatenate([gated, jnp.zeros((PAD - TOK, D), F32)], axis=0).astype(BF16)
            send(back_send, back_recv, pass_send.at[1], pass_recv.at[1], twin, col)
        else:
            out_ref[core] = (token_in_ref[core] + dot(gated.astype(BF16), weights_ref[4])).astype(BF16)

    attend(keys_ref, vt_ref, bias_of, qt_ref, scores_ref, p_ref, mix_ref, after_slab)
    wait(back_recv, pass_send.at[1], pass_recv.at[1], twin, col)
    out_ref[1 - core] = (token_in_ref[1 - core] + dot(back_recv[...], weights_ref[4])[:TOK]).astype(BF16)
    for copy in sent:
        copy.wait_send()


def shards(atom_feat, atom_token, pair_cond, token_mask, atom_wq, atom_wk, atom_wv, atom_wo, agg_weight, pair_weight,
           token_gain, query_weight, key_weight, value_weight, gate_weight, out_weight):
    whole = ATOMS + 2 * RIM
    dma = pltpu.SemaphoreType.DMA
    here, there = pl.BlockSpec(memory_space=pltpu.VMEM), pl.BlockSpec(memory_space=pl.ANY)
    return pl.pallas_call(
        whole_kernel,
        out_shape=jax.ShapeDtypeStruct((2, TOK, D), BF16),
        in_specs=[here] * 11 + [there] * 5,
        out_specs=here,
        scratch_shapes=[
            pltpu.VMEM((LANES, 128), F32), pltpu.VMEM((2, 2, RIM, CA), BF16), pltpu.VMEM((whole, CA), BF16),
            pltpu.VMEM((ATOMS, CA), BF16), pltpu.VMEM((whole, CA), BF16), pltpu.VMEM((whole, 2 * CA), BF16),
            pltpu.VMEM((ATOMS, CA), BF16), pltpu.VMEM((2, TOK, D), F32), pltpu.VMEM((PAD, D), BF16),
            pltpu.VMEM((2, 8, PAD, D), BF16), pltpu.VMEM((2, 2, 8, PAD, LANES), BF16), pltpu.VMEM((5, D, D), BF16),
            pltpu.VMEM((D, D), BF16), pltpu.VMEM((KEYS, D), BF16), pltpu.VMEM((D, KEYS), BF16),
            pltpu.VMEM((2, D, TOK), BF16), pltpu.VMEM((2, TOK, D), F32), pltpu.VMEM((2, KEYS, 256), F32),
            pltpu.VMEM((2, KEYS, 256), BF16), pltpu.VMEM((2, TOK, D), F32), pltpu.VMEM((PAD, D), BF16),
            pltpu.VMEM((PAD, D), BF16), dma((5,)), dma((2,)), dma((2,)), dma((20,)), dma((20,)), dma((4,)), dma((4,)),
            dma((18,)), dma((18,)), dma((2,)), dma((2,)),
        ],
        compiler_params=pltpu.CompilerParams(collective_id=0, has_side_effects=True, vmem_limit_bytes=60 * 1024 * 1024),
        name="whole",
    )(pair_cond, token_mask.reshape(1, TOK), pair_weight.T, atom_feat, atom_token.reshape(1, ATOMS), atom_wq, atom_wk,
      atom_wv, atom_wo, agg_weight, token_gain.reshape(1, D), query_weight, key_weight, value_weight, gate_weight, out_weight)


def solution(mesh):
    placed = (P("sample", "row", None), P("row"), P("row", "sample", None), P("sample")) + (P(),) * 12
    return jax.shard_map(shards, mesh=mesh, in_specs=placed, out_specs=P("sample", "row", None), check_vma=False)
```

time: 218 us -> 70.1 us (0.32)
  waiting for transfers between devices: 104 us -> 0 us
  Pallas kernels: 0 us -> 65.7 us
  matrix products: 37.7 us -> 0 us
  local copies, waits for them, and re-layouts: 34.8 us -> 4.2 us
  other arithmetic: 20.3 us -> 0 us
  between operations: 13.6 us -> 0.01 us
  starting transfers between devices: 7.52 us -> 0 us
    all_gather x3 -> x0, waiting for transfers between devices: 104 us -> none  [the longest x1 49.5 us: shards(): bias_rows = lax.all_gather(bias_part, 'sample', axis=2, tiled=True)]
    pallas_call x0 -> x1, Pallas kernels: none -> 65.7 us  [shards(): pl.pallas_call(whole_kernel, out_shape=jax.ShapeDtypeStruct((2, TOK, D),...]
    dot_general x14 -> x0, matrix products: 37.7 us -> none  [the longest x1 9.51 us: shards(): jnp.einsum('shqk,skhd->shqd', expd.astype(jnp.bfloat16), attend_tvals, pr...]
    all_gather x3 -> x0, local copies, waits for them, and re-layouts: 18.2 us -> none  [the longest x1 6.6 us: shards(): bias_rows = lax.all_gather(bias_part, 'sample', axis=2, tiled=True)]
    reduce_sum x8 -> x0, other arithmetic: 12.6 us -> none  [the longest x3 4.26 us: layer_norm(): var = jnp.mean(centre * centre, -1, keepdims=True)]
    convert_element_type x4 -> x0, local copies, waits for them, and re-layouts: 7.34 us -> none  [the longest x2 6 us: shards(): jnp.transpose(amix, (0, 1, 3, 2, 4)).reshape(samples, atoms, chans)]
    ppermute x2 -> x0, starting transfers between devices: 7.04 us -> none  [the longest x1 4.94 us: with_halo(): before = lax.ppermute(last, axis, up)]
    convert_element_type x2 -> x0, other arithmetic: 6.22 us -> none  [the longest x1 4.47 us: shards(): tbias = bias_rows.astype(jnp.float32)]
  transfers between devices with their start and end apart: 5 -> 0, of which waited for: 3 -> 0; matrix products, arithmetic and copies ran while one was open for 31% -> 0% of each run, Pallas kernels for 0% -> 0%
where the time goes in v1:
time: 70.1 us; the launch traced here: 69.9 us
  Pallas kernels  65.7 us (94%)
  local copies, waits for them, and re-layouts  4.2 us (6%)
    pallas_call x1, Pallas kernels, shards(): pl.pallas_call(whole_kernel, out_shape=jax.ShapeDtypeStruct((2, TOK, D),...  65.7 us
    unnamed x1, local copies, waits for them, and re-layouts  1.64 us

profile of v1, /device:TPU:1, one launch (start us, length us, event | category | flops | bytes accessed | tf_op | source)
XLA Modules:
  0.0 69.9 jit_solution(11396117819965683494)
XLA Ops:
  0.0 1.3 %reshape.11.gain_ref = f32[1,768]{1,0:T(1,128)} reshape(f32[768]{0:T(1024)} %param.26) | data formatting | bytes 6144 | tf_op jit(solution)/shard_map/reshape | solution.py:425
  1.3 1.3 %reshape.10.token_ref = s32[1,1152]{1,0:T(1,128)} reshape(s32[1152]{0:T(1024)} %param.17) | data formatting | bytes 9216 | tf_op jit(solution)/shard_map/reshape | solution.py:424
  2.6 65.7 %whole.1 = bf16[2,72,768]{2,1,0:T(8,128)(2,1)} custom-call(bf16[72,72,128]{2,1,0:T(8,128)(2,1)} %pair_ref.1, s32[1,72]{1,0:T(1,128)} %bitcast.3, bf16[16,128]{1,0:T(8,128)(2,1)} %bitcast.2, bf16[2,1152,128]{2,1,0:T(8,128)(2,1)} %feat_ref.1, s32[1,1152]{1,0:T(1,128)} %reshape.10.token_ref, bf16[128,128]{1,0:T(8,128)(2,1)} %wq.1, bf16[128,128]{1,0:T(8,128)(2,1)} %wk.1, ...), custom_call_target="tpu_custom_call" | custom-call | tf_op jit(solution)/shard_map/whole/pallas_call | solution.py:406
  68.2 1.6 %copy.18 = bf16[2,72,768]{2,1,0:T(8,128)(2,1)} copy(bf16[2,72,768]{2,1,0:T(8,128)(2,1)} %whole.1) | data formatting | bytes 442368

commit v2 on v1

v2 whole, which is shorter than its diff:
```python
import jax
import jax.numpy as jnp
from jax import lax
from jax.experimental import pallas as pl
from jax.experimental.pallas import tpu as pltpu
from jax.sharding import PartitionSpec as P

HEADS = 16
HEAD_DIM = 48
AHEADS = 4
AHEAD_DIM = 32
QWIN = 32
KWIN = 128
RIM = 48
TOK = 72
PAD = 80
ATOMS = 1152
CA = 128
D = 768
LANES = HEADS * TOK
F32 = jnp.float32
BF16 = jnp.bfloat16
NEG = -1e30
CHUNKS = ((0, 256, 0, 256), (256, 256, 128, 256), (512, 256, 256, 384), (768, 128, 384, 256), (896, 256, 512, 256))


def dot(a, b):
    return jnp.dot(a, b, preferred_element_type=F32)


def dot_nt(a, b):
    return lax.dot_general(a, b, (((1,), (1,)), ((), ())), preferred_element_type=F32)


def layer_norm(x):
    mean = jnp.mean(x, -1, keepdims=True)
    centre = x - mean
    var = jnp.mean(centre * centre, -1, keepdims=True)
    return centre * lax.rsqrt(var + 1e-05)


def iota(shape, dim):
    return lax.broadcasted_iota(jnp.int32, shape, dim)


MESH = pl.DeviceIdType.MESH
KEYS = 16 * PAD
PAIR_ROWS = 12
HALF = 8 * PAD
GROUPS = ((0, 512), (512, 384), (896, 256))
WORK = ((1, 0), (1, 1), (0, 0), (0, 1), (1, 2), (1, 3), (0, 2), (0, 3), (0, 4), (1, 4))
PARTS = ((0, 48), (48, 32))


def pair_part(pair_load, pair_ref, mask_ref, weight_ref, table_ref, out, row, col, unroll=24):
    weight_t = weight_ref[...]

    def step(g, carry):
        for n in range(unroll // PAIR_ROWS):
            pair_load(g * (unroll // PAIR_ROWS) + n).wait()
        normed = [layer_norm(pair_ref[g * unroll + u].astype(F32)).astype(BF16) for u in range(unroll)]
        raw = [dot_nt(weight_t, n) for n in normed]
        for u in range(unroll):
            table_ref[pl.ds(g * unroll + u, HEADS, stride=TOK), :TOK] = raw[u]
        return carry

    lax.fori_loop(0, TOK // unroll, step, 0)
    kidx = col * TOK + iota((TOK, TOK), 1)
    qidx = row * TOK + iota((TOK, TOK), 0)
    allowed = (mask_ref[...][None, :] == 1) | (qidx == kidx)
    for h in range(HEADS):
        rows = pl.ds(h * TOK, TOK)
        table_ref[rows, :TOK] = jnp.where(allowed, table_ref[rows, :TOK], -30000.0)
    for n in range(LANES // 128):
        part = table_ref[n * 128 : (n + 1) * 128, :].T[:TOK]
        filled = jnp.concatenate([part, jnp.full((PAD - TOK, 128), NEG, F32)], axis=0)
        out[:, n * 128 : (n + 1) * 128] = filled.astype(BF16)


def atom_project(s, feat_ref, wq, wk, wv, q_ref, k_ref, v_ref):
    for c in range(3):
        normed = layer_norm(feat_ref[s, c * 384 : (c + 1) * 384].astype(F32)).astype(BF16)
        here = pl.ds(RIM + c * 384, 384)
        k_ref[s, here, :] = dot(normed, wk).astype(BF16)
        v_ref[s, here, :CA] = dot(normed, wv).astype(BF16)
        v_ref[s, here, CA:] = jnp.ones((384, CA), BF16)
        q_ref[s, pl.ds(c * 384, 384), :] = dot(normed, wq).astype(BF16)


def atom_rim(s, halo_ref, wk, wv, k_ref, v_ref, row, rows):
    last = RIM + ATOMS
    first_key = k_ref[s, RIM : RIM + 16, :].astype(F32)[:1]
    last_key = k_ref[s, last - 16 : last, :].astype(F32)[15:]
    for side, outside, start, key in ((0, row == 0, 0, first_key), (1, row == rows - 1, last, last_key)):
        normed = layer_norm(halo_ref[side, s].astype(F32)).astype(BF16)
        here = pl.ds(start, RIM)
        k_ref[s, here, :] = jnp.where(outside, jnp.broadcast_to(key, (RIM, CA)), dot(normed, wk)).astype(BF16)
        v_ref[s, here, :CA] = jnp.where(outside, 0.0, dot(normed, wv)).astype(BF16)
        v_ref[s, here, CA:] = jnp.where(outside, 0.0, jnp.ones((RIM, CA), F32)).astype(BF16)


def atom_windows(s, windows, q_ref, k_ref, v_ref, att_ref):
    head_of = iota((AHEADS * QWIN, CA), 0) // QWIN == iota((AHEADS * QWIN, CA), 1) // AHEAD_DIM
    lane_head = iota((QWIN, CA), 1) // AHEAD_DIM
    factor = 1.4426950408889634 / AHEAD_DIM**0.5
    starts = [w * QWIN for w in windows]
    scores = []
    for start in starts:
        q = q_ref[s, pl.ds(start, QWIN), :]
        stacked = jnp.where(head_of, jnp.concatenate([q] * AHEADS, axis=0), jnp.zeros((), BF16))
        scores.append(dot_nt(stacked, k_ref[s, pl.ds(start, KWIN), :]))
    exps = [jnp.exp2((sc - jnp.max(sc, -1, keepdims=True)) * factor).astype(BF16) for sc in scores]
    for start, e in zip(starts, exps):
        both = dot(e, v_ref[s, pl.ds(start, KWIN), :])
        top, low = both[:QWIN, :CA], both[:QWIN, CA:]
        for h in range(1, AHEADS):
            here = slice(h * QWIN, (h + 1) * QWIN)
            top = jnp.where(lane_head == h, both[here, :CA], top)
            low = jnp.where(lane_head == h, both[here, CA:], low)
        att_ref[s, pl.ds(start, QWIN), :] = (top / low).astype(BF16)


def atom_sum(s, chunks, feat_ref, token_ref, wo, agg_ref, att_ref, row):
    total = jnp.zeros((TOK, D), F32)
    for start, size in chunks:
        here = pl.ds(start, size)
        out = (feat_ref[s, here, :].astype(F32) + dot(att_ref[s, here, :], wo)).astype(BF16)
        hidden = jnp.maximum(dot(out, agg_ref[...]), 0.0).astype(BF16)
        onehot = token_ref[start : start + size][None, :] - row * TOK == iota((TOK, size), 0)
        total += dot(onehot.astype(BF16), hidden)
    return total


def token_counts(token_ref, row):
    onehot = token_ref[...][None, :] - row * TOK == iota((TOK, ATOMS), 0)
    return jnp.sum(onehot.astype(F32), -1, keepdims=True)


def token_norm(token_in, gain_ref):
    tnorm = layer_norm(token_in) * gain_ref[...][None, :]
    return jnp.concatenate([tnorm, jnp.zeros((PAD - TOK, D), F32)], axis=0).astype(BF16)


def query_prep(qt_ref, slab, chunk):
    lo, width, clo, cwidth = chunk
    lane = lo + iota((TOK, width), 1)
    fold = (lane % TOK == iota((TOK, width), 0)).astype(BF16)
    own_head = (lo + iota((cwidth, width), 1)) // TOK == (clo + iota((cwidth, width), 0)) // HEAD_DIM
    query = jnp.where(own_head, dot(qt_ref[slab, pl.ds(clo, cwidth), :], fold), 0.0).astype(BF16)
    return fold, own_head, query


def attend(k_ref, vt_ref, bias_of, qt_ref, scores_ref, p_ref, mix_ref, before, after_slab, blk=PAD * 2):
    mix_ref[...] = jnp.zeros_like(mix_ref)
    work = [(slab, CHUNKS[c]) for slab, c in WORK]
    blocks = KEYS // blk
    state = {}
    for i in range(len(work) + 2):
        before(i)
        now = work[i] if i < len(work) else None
        exps = work[i - 1] if 0 <= i - 1 < len(work) else None
        vals = work[i - 2] if i >= 2 else None
        if exps:
            top = jnp.max(state[i - 1][3], axis=0, keepdims=True)
            total = jnp.zeros((8, exps[1][1]), F32)
        if now:
            lo, width, clo, cwidth = now[1]
            state[i] = list(query_prep(qt_ref, *now)) + [jnp.full((8, width), -3e38, F32)]
            ahead = dot(k_ref[0:blk, clo : clo + cwidth], state[i][2])
        if vals:
            _, vwidth, vlo, vcwidth = vals[1]
            out = dot(vt_ref[pl.ds(vlo, vcwidth), :], p_ref[i % 2, :, :vwidth])
        for b in range(blocks):
            here = pl.ds(b * blk, blk)
            if now:
                raw = ahead
                if b + 1 < blocks:
                    ahead = dot(k_ref[(b + 1) * blk : (b + 2) * blk, clo : clo + cwidth], state[i][2])
            if exps:
                ewidth = exps[1][1]
                e = jnp.exp(scores_ref[(i - 1) % 2, here, :ewidth] - top)
                total += jnp.sum(e.reshape(blk // 8, 8, ewidth), axis=0)
                p_ref[(i - 1) % 2, here, :ewidth] = e.astype(BF16)
            if now:
                sc = raw * (1.0 / HEAD_DIM**0.5) + bias_of(now[0], b, blk, lo, width)
                scores_ref[i % 2, here, :width] = sc
                state[i][3] = jnp.maximum(state[i][3], jnp.max(sc.reshape(blk // 8, 8, width), axis=0))
        if exps:
            state[i - 1].append(jnp.sum(total, axis=0, keepdims=True))
        if vals:
            fold, own_head, _, _, vsum = state.pop(i - 2)
            out = jnp.where(own_head, out * (1.0 / vsum), 0.0)
            high = out.astype(BF16)
            rest = (out - high.astype(F32)).astype(BF16)
            mix_ref[vals[0], :, vlo : vlo + vcwidth] += dot_nt(fold, high) + dot_nt(fold, rest)
            if vals[1] == CHUNKS[-1]:
                after_slab(vals[0])


def whole_kernel(mask_ref, pair_w_ref, token_ref, wq, wk, wv, wo, gain_ref, pair_hbm, feat_hbm, agg_hbm,
                 query_hbm, key_hbm, value_hbm, gate_hbm, out_hbm, out_ref,
                 pair_ref, feat_ref, agg_ref, table_ref, halo_ref, q_ref, k_ref, v_ref, att_ref, token_in_ref, counts_ref, give_ref, tall_ref, bias_ref,
                 weights_ref, wvt_ref, keys_ref, vt_ref, qt_ref, sig_ref, scores_ref, p_ref, mix_ref, back_send, back_recv,
                 load_sem, halo_send, halo_recv, bias_send, bias_recv, twin_send, twin_recv, tok_send, tok_recv,
                 pass_send, pass_recv):
    row, col = lax.axis_index("row"), lax.axis_index("sample")
    rows, cols = lax.axis_size("row"), lax.axis_size("sample")
    core, zl, y = row % 2, (row // 2) % 2, row // 4
    x, zh = col % 4, col // 4
    twin, zpair = row + 1 - 2 * core, row + 2 - 4 * zl
    y_up, y_down = (row + 4) % rows, (row + rows - 4) % rows
    r_up, r_down = (row + 1) % rows, (row + rows - 1) % rows
    x_up, x_down = zh * 4 + (x + 1) % 4, zh * 4 + (x + 3) % 4
    z_up, z_down = (col + 4) % cols, (col + cols - 4) % cols
    def pair_load(n):
        here = pl.ds(n * PAIR_ROWS, PAIR_ROWS)
        return pltpu.make_async_copy(pair_hbm.at[here], pair_ref.at[here], load_sem.at[n])

    first = TOK // PAIR_ROWS
    for n in range(first):
        pair_load(n).start()
    sources = [(feat_hbm.at[0], feat_ref.at[0]), (feat_hbm.at[1], feat_ref.at[1]), (agg_hbm, agg_ref)]
    sources += [(source, weights_ref.at[n]) for n, source in enumerate((query_hbm, key_hbm, value_hbm, gate_hbm, out_hbm))]
    loads = [pltpu.make_async_copy(*pair, load_sem.at[first + n]) for n, pair in enumerate(sources)]
    for load in loads:
        load.start()

    barrier = pltpu.get_barrier_semaphore()
    for peer in (twin, zpair, y_up, y_down, r_up, r_down):
        pl.semaphore_signal(barrier, inc=1, device_id=(peer, col), device_id_type=MESH)
    for peer in (x_up, x_down, z_up, z_down):
        pl.semaphore_signal(barrier, inc=1, device_id=(row, peer), device_id_type=MESH)

    sent = []

    def send(src, dst, send_sem, recv_sem, peer_row, peer_col):
        copy = pltpu.make_async_remote_copy(src_ref=src, dst_ref=dst, send_sem=send_sem, recv_sem=recv_sem,
                                            device_id=(peer_row, peer_col), device_id_type=MESH)
        copy.start()
        sent.append(copy)

    def wait(dst, send_sem, recv_sem, peer_row, peer_col):
        pltpu.make_async_remote_copy(src_ref=dst, dst_ref=dst, send_sem=send_sem, recv_sem=recv_sem,
                                     device_id=(peer_row, peer_col), device_id_type=MESH).wait_recv()

    z_order = (zh, (zh + 3) % 4, (zh + 1) % 4, (zh + 2) % 4)

    def slot(g, zb, xb, part):
        rows_here = pl.ds(*part) if part else pl.ds(0, PAD)
        return bias_ref.at[core, xb % 2, zb, xb // 2, rows_here, pl.ds(*GROUPS[g])]

    def got(g, role, zb, xb, part=None):
        n = g * 20 + role
        wait(slot(g, zb, xb, part), bias_send.at[n], bias_recv.at[n], row, col)

    def give(g, role, zb, xb, peer, part=None):
        at, n = slot(g, zb, xb, part), g * 20 + role
        send(at, at, bias_send.at[n], bias_recv.at[n], row, peer)

    def z_own(g):
        give(g, 0, zh, x, z_up)
        give(g, 1, zh, x, z_down)

    def z_pass(g, way):
        got(g, way, z_order[1 + way], x)
        give(g, 2 + way, z_order[1 + way], x, z_down if way else z_up, PARTS[way])

    def z_end(g):
        got(g, 2, z_order[3], x, PARTS[0])
        got(g, 3, z_order[3], x, PARTS[1])

    def x_own(g, j):
        give(g, 4 + 4 * j, z_order[j], x, x_up)
        give(g, 5 + 4 * j, z_order[j], x, x_down)

    def x_pass(g, j, way):
        parts = PARTS if j % 2 else PARTS[::-1]
        origin = (x + 1) % 4 if way else (x + 3) % 4
        got(g, 4 + 4 * j + way, z_order[j], origin)
        give(g, 6 + 4 * j + way, z_order[j], origin, x_down if way else x_up, parts[way])

    def x_end(g, j):
        first, second = PARTS if j % 2 else PARTS[::-1]
        got(g, 6 + 4 * j, z_order[j], (x + 2) % 4, first)
        got(g, 7 + 4 * j, z_order[j], (x + 2) % 4, second)
        at, n = bias_ref.at[core, :, z_order[j], :, :, pl.ds(*GROUPS[g])], g * 4 + j
        send(at, at, twin_send.at[n], twin_recv.at[n], twin, col)

    def twin_end(g):
        for j in range(4):
            n = g * 4 + j
            at = bias_ref.at[1 - core, :, z_order[j], :, :, pl.ds(*GROUPS[g])]
            wait(at, twin_send.at[n], twin_recv.at[n], twin, col)

    def tok_slot(late, yb, zb, part=None):
        at = tall_ref.at[core if late else 1 - core, yb * 2 + zb]
        return at if part is None else at.at[pl.ds(*part)]

    def tok_wait(late, role, yb, zb, part=None):
        n = late * 9 + role
        wait(tok_slot(late, yb, zb, part), tok_send.at[n], tok_recv.at[n], row, col)

    def tok_give(late, role, yb, zb, peer, part=None):
        at, n = tok_slot(late, yb, zb, part), late * 9 + role
        send(at, at, tok_send.at[n], tok_recv.at[n], peer, col)

    zs = (zl, 1 - zl)

    def tok_own(late):
        tok_give(late, 0, y, zl, zpair)
        tok_give(late, 1, y, zl, y_up)
        tok_give(late, 2, y, zl, y_down)

    def tok_second(late):
        tok_wait(late, 0, y, 1 - zl)
        tok_give(late, 5, y, 1 - zl, y_up)
        tok_give(late, 6, y, 1 - zl, y_down)

    def tok_pass(late, j, way):
        origin = (y + 1) % 4 if way else (y + 3) % 4
        tok_wait(late, 1 + 4 * j + way, origin, zs[j])
        tok_give(late, 3 + 4 * j + way, origin, zs[j], y_down if way else y_up, PARTS[way])

    def tok_end(late):
        for j in range(2):
            tok_wait(late, 3 + 4 * j, (y + 2) % 4, zs[j], PARTS[0])
            tok_wait(late, 4 + 4 * j, (y + 2) % 4, zs[j], PARTS[1])

    def windows(s, which):
        atom_windows(s, which, q_ref, k_ref, v_ref, att_ref)

    def inner(s):
        token_in_ref[s] = atom_sum(s, ((128, 384), (512, 384), (896, 128)), feat_ref, token_ref, wo[...], agg_ref, att_ref,
                                   row)

    def tokens(s):
        edges = atom_sum(s, ((0, 128), (1024, 128)), feat_ref, token_ref, wo[...], agg_ref, att_ref, row)
        token_in = (token_in_ref[s] + edges) / counts_ref[:, :1]
        token_in_ref[s] = token_in
        return token_norm(token_in, gain_ref)

    def rim(s):
        atom_rim(s, halo_ref, wk[...], wv[...], k_ref, v_ref, row, rows)
        windows(s, (0, 1, ATOMS // QWIN - 2, ATOMS // QWIN - 1))

    pair_part(pair_load, pair_ref, mask_ref, pair_w_ref, table_ref, bias_ref.at[core, x % 2, zh, x // 2], row, col)
    loads[0].wait()
    loads[1].wait()
    for s in (1 - core, core):
        atom_project(s, feat_ref, wq[...], wk[...], wv[...], q_ref, k_ref, v_ref)
        for lo, hi in ((2, 14), (14, 26), (26, 34)):
            windows(s, range(lo, hi))

    pl.semaphore_wait(barrier, 10)
    send(feat_hbm.at[:, ATOMS - RIM :], halo_ref.at[0], halo_send.at[0], halo_recv.at[0], r_up, col)
    send(feat_hbm.at[:, :RIM], halo_ref.at[1], halo_send.at[1], halo_recv.at[1], r_down, col)

    def project_tokens(which):
        base = pl.multiple_of(which * HALF, HALF)
        block = tall_ref[which].reshape(HALF, D)
        keys_ref[pl.ds(base, HALF), :] = dot(block, weights_ref[1]).astype(BF16)
        vt_ref[:, pl.ds(base, HALF)] = dot_nt(wvt_ref[...], block).astype(BF16)

    z_own(0)
    x_own(0, 0)
    counts_ref[...] = jnp.broadcast_to(token_counts(token_ref, row), (TOK, 128))
    loads[2].wait()
    inner(1 - core)
    inner(core)
    for load in loads[3:]:
        load.wait()
    wvt_ref[...] = weights_ref[2].astype(F32).T.astype(BF16)
    x_own(1, 0)
    x_own(2, 0)
    z_own(1)
    wait(halo_ref.at[0], halo_send.at[0], halo_recv.at[0], r_up, col)
    wait(halo_ref.at[1], halo_send.at[1], halo_recv.at[1], r_down, col)
    rim(1 - core)
    give_ref[...] = tokens(1 - core)
    send(give_ref, tall_ref.at[core, y * 2 + zl], pass_send.at[0], pass_recv.at[0], twin, col)
    rim(core)
    tall_ref[core, y * 2 + zl] = tokens(core)
    tok_own(1)
    x_pass(0, 0, 0)
    x_pass(0, 0, 1)
    wait(tall_ref.at[1 - core, y * 2 + zl], pass_send.at[0], pass_recv.at[0], twin, col)
    tok_own(0)
    for slab in range(2):
        block = tall_ref[core if slab else 1 - core, y * 2 + zl]
        qt_ref[slab] = dot(block, weights_ref[0])[:TOK].T.astype(BF16)
        sig_ref[slab] = jax.nn.sigmoid(dot(block, weights_ref[3])[:TOK])
    x_pass(1, 0, 0)
    x_pass(1, 0, 1)
    x_pass(2, 0, 0)
    x_pass(2, 0, 1)
    z_pass(0, 0)
    x_own(0, 1)
    z_pass(0, 1)
    x_own(0, 2)
    x_end(0, 0)
    z_pass(1, 0)
    z_pass(1, 1)
    x_end(1, 0)
    x_own(1, 1)
    tok_pass(1, 0, 0)
    tok_pass(1, 0, 1)
    x_end(2, 0)
    tok_second(1)
    x_own(1, 2)
    x_pass(0, 1, 0)
    x_pass(0, 1, 1)
    tok_pass(0, 0, 0)
    tok_pass(0, 0, 1)
    x_pass(0, 2, 0)
    z_own(2)
    tok_second(0)
    x_pass(0, 2, 1)
    x_pass(1, 1, 0)
    x_pass(1, 1, 1)
    x_pass(1, 2, 0)
    tok_pass(1, 1, 1)
    x_pass(1, 2, 1)
    tok_pass(1, 1, 0)
    z_end(0)
    x_own(0, 3)
    x_end(0, 1)
    x_end(0, 2)
    z_end(1)
    x_own(1, 3)
    x_end(1, 1)
    z_pass(2, 1)
    x_own(2, 2)
    x_end(1, 2)
    tok_pass(0, 1, 1)
    z_pass(2, 0)
    x_own(2, 1)
    tok_pass(0, 1, 0)
    x_pass(0, 3, 0)
    x_pass(0, 3, 1)
    x_pass(1, 3, 0)
    x_pass(1, 3, 1)
    x_pass(2, 2, 0)
    x_pass(2, 2, 1)
    x_pass(2, 1, 0)
    x_pass(2, 1, 1)
    z_end(2)
    x_own(2, 3)
    tok_end(0)
    project_tokens(1 - core)
    x_end(0, 3)
    x_end(1, 3)
    x_end(2, 2)
    tok_end(1)
    project_tokens(core)
    x_pass(2, 3, 0)
    x_pass(2, 3, 1)
    x_end(2, 1)

    def before(i):
        if i == 2:
            twin_end(0)
        if i == 4:
            x_end(2, 3)
        if i == 6:
            twin_end(1)
        if i == 8:
            twin_end(2)

    def bias_of(slab, b, blk, lo, width):
        first = b * (blk // PAD)
        at = bias_ref[core if slab else 1 - core, first // 8, first % 8 // 2, :, :, lo : lo + width]
        return at.astype(F32).reshape(blk, width)

    def after_slab(slab):
        gated = mix_ref[slab] * sig_ref[slab]
        if slab == 0:
            back_send[...] = jnp.concatenate([gated, jnp.zeros((PAD - TOK, D), F32)], axis=0).astype(BF16)
            send(back_send, back_recv, pass_send.at[1], pass_recv.at[1], twin, col)
        else:
            out_ref[core] = (token_in_ref[core] + dot(gated.astype(BF16), weights_ref[4])).astype(BF16)

    attend(keys_ref, vt_ref, bias_of, qt_ref, scores_ref, p_ref, mix_ref, before, after_slab)
    wait(back_recv, pass_send.at[1], pass_recv.at[1], twin, col)
    out_ref[1 - core] = (token_in_ref[1 - core] + dot(back_recv[...], weights_ref[4])[:TOK]).astype(BF16)
    for copy in sent:
        copy.wait_send()


def shards(atom_feat, atom_token, pair_cond, token_mask, atom_wq, atom_wk, atom_wv, atom_wo, agg_weight, pair_weight,
           token_gain, query_weight, key_weight, value_weight, gate_weight, out_weight):
    whole = ATOMS + 2 * RIM
    dma = pltpu.SemaphoreType.DMA
    here, there = pl.BlockSpec(memory_space=pltpu.VMEM), pl.BlockSpec(memory_space=pl.ANY)
    return pl.pallas_call(
        whole_kernel,
        out_shape=jax.ShapeDtypeStruct((2, TOK, D), BF16),
        in_specs=[here] * 8 + [there] * 8,
        out_specs=here,
        scratch_shapes=[
            pltpu.VMEM((TOK, TOK, 128), BF16), pltpu.VMEM((2, ATOMS, CA), BF16), pltpu.VMEM((CA, D), BF16),
            pltpu.VMEM((LANES, 128), F32), pltpu.VMEM((2, 2, RIM, CA), BF16),
            pltpu.VMEM((2, ATOMS, CA), BF16), pltpu.VMEM((2, whole, CA), BF16), pltpu.VMEM((2, whole, 2 * CA), BF16),
            pltpu.VMEM((2, ATOMS, CA), BF16), pltpu.VMEM((2, TOK, D), F32), pltpu.VMEM((TOK, 128), F32), pltpu.VMEM((PAD, D), BF16),
            pltpu.VMEM((2, 8, PAD, D), BF16), pltpu.VMEM((2, 2, 4, 2, PAD, LANES), BF16), pltpu.VMEM((5, D, D), BF16),
            pltpu.VMEM((D, D), BF16), pltpu.VMEM((KEYS, D), BF16), pltpu.VMEM((D, KEYS), BF16),
            pltpu.VMEM((2, D, TOK), BF16), pltpu.VMEM((2, TOK, D), F32), pltpu.VMEM((2, KEYS, 256), F32),
            pltpu.VMEM((2, KEYS, 256), BF16), pltpu.VMEM((2, TOK, D), F32), pltpu.VMEM((PAD, D), BF16),
            pltpu.VMEM((PAD, D), BF16), dma((14,)), dma((2,)), dma((2,)), dma((60,)), dma((60,)), dma((12,)), dma((12,)),
            dma((18,)), dma((18,)), dma((2,)), dma((2,)),
        ],
        compiler_params=pltpu.CompilerParams(collective_id=0, has_side_effects=True, vmem_limit_bytes=60 * 1024 * 1024),
        name="whole",
    )(token_mask, pair_weight.T, atom_token, atom_wq, atom_wk, atom_wv, atom_wo, token_gain, pair_cond, atom_feat,
      agg_weight, query_weight, key_weight, value_weight, gate_weight, out_weight)


def solution(mesh):
    placed = (P("sample", "row", None), P("row"), P("row", "sample", None), P("sample")) + (P(),) * 12
    return jax.shard_map(shards, mesh=mesh, in_specs=placed, out_specs=P("sample", "row", None), check_vma=False)
```

time: 70.1 us -> 61.5 us (0.88)
  Pallas kernels: 65.7 us -> 59.7 us
  local copies, waits for them, and re-layouts: 4.2 us -> 1.64 us
    pallas_call x1, Pallas kernels: 65.7 us -> 59.7 us  [shards(): pl.pallas_call(whole_kernel, out_shape=jax.ShapeDtypeStruct((2, TOK, D),...]
    reshape x2 -> x0, local copies, waits for them, and re-layouts: 2.57 us -> none  [the longest x1 1.29 us: shards(): atom_token.reshape(1, ATOMS)]
where the time goes in v2:
time: 61.5 us; the launch traced here: 61.4 us
  Pallas kernels  59.7 us (97%)
  local copies, waits for them, and re-layouts  1.64 us (3%)
    pallas_call x1, Pallas kernels, shards(): pl.pallas_call(whole_kernel, out_shape=jax.ShapeDtypeStruct((2, TOK, D),...  59.7 us
    unnamed x1, local copies, waits for them, and re-layouts  1.64 us

profile of v2, /device:TPU:1, one launch (start us, length us, event | category | flops | bytes accessed | tf_op | source)
XLA Modules:
  0.0 61.4 jit_solution(2911201565265411081)
XLA Ops:
  0.0 59.7 %whole.1 = bf16[2,72,768]{2,1,0:T(8,128)(2,1)} custom-call(s32[72]{0:T(128)} %mask_ref.1, bf16[16,128]{1,0:T(8,128)(2,1)} %bitcast.1, s32[1152]{0:T(1024)} %token_ref.1, bf16[128,128]{1,0:T(8,128)(2,1)} %wq.1, bf16[128,128]{1,0:T(8,128)(2,1)} %wk.1, bf16[128,128]{1,0:T(8,128)(2,1)} %wv.1, bf16[128,128]{1,0:T(8,128)(2,1)} %wo.1, f32[768]{0:T(1024)} %gain_ref.1, ...), custom_call_target="tpu_custom_call" | custom-call | tf_op jit(solution)/shard_map/whole/pallas_call | solution.py:494
  59.7 1.6 %copy.18 = bf16[2,72,768]{2,1,0:T(8,128)(2,1)} copy(bf16[2,72,768]{2,1,0:T(8,128)(2,1)} %whole.1) | data formatting | bytes 442368

commit v3 on v2

--- a/solution.py
+++ b/solution.py
@@ -47,8 +47,8 @@
 KEYS = 16 * PAD
 PAIR_ROWS = 12
 HALF = 8 * PAD
-GROUPS = ((0, 512), (512, 384), (896, 256))
-WORK = ((1, 0), (1, 1), (0, 0), (0, 1), (1, 2), (1, 3), (0, 2), (0, 3), (0, 4), (1, 4))
+GROUPS = ((0, 256), (256, 512), (768, 384))
+WORK = ((1, 0), (0, 0), (1, 1), (1, 2), (0, 1), (0, 2), (1, 3), (0, 3), (0, 4), (1, 4))
 PARTS = ((0, 48), (48, 32))
 
 
@@ -366,104 +366,104 @@
     counts_ref[...] = jnp.broadcast_to(token_counts(token_ref, row), (TOK, 128))
     loads[2].wait()
     inner(1 - core)
+    z_own(1)
+    x_own(1, 0)
     inner(core)
     for load in loads[3:]:
         load.wait()
     wvt_ref[...] = weights_ref[2].astype(F32).T.astype(BF16)
-    x_own(1, 0)
     x_own(2, 0)
-    z_own(1)
     wait(halo_ref.at[0], halo_send.at[0], halo_recv.at[0], r_up, col)
     wait(halo_ref.at[1], halo_send.at[1], halo_recv.at[1], r_down, col)
     rim(1 - core)
+    x_pass(0, 0, 0)
+    x_pass(0, 0, 1)
     give_ref[...] = tokens(1 - core)
     send(give_ref, tall_ref.at[core, y * 2 + zl], pass_send.at[0], pass_recv.at[0], twin, col)
     rim(core)
     tall_ref[core, y * 2 + zl] = tokens(core)
     tok_own(1)
-    x_pass(0, 0, 0)
-    x_pass(0, 0, 1)
+    z_pass(0, 0)
+    z_pass(0, 1)
     wait(tall_ref.at[1 - core, y * 2 + zl], pass_send.at[0], pass_recv.at[0], twin, col)
     tok_own(0)
+    x_own(0, 1)
     for slab in range(2):
         block = tall_ref[core if slab else 1 - core, y * 2 + zl]
         qt_ref[slab] = dot(block, weights_ref[0])[:TOK].T.astype(BF16)
         sig_ref[slab] = jax.nn.sigmoid(dot(block, weights_ref[3])[:TOK])
+    x_own(0, 2)
     x_pass(1, 0, 0)
     x_pass(1, 0, 1)
     x_pass(2, 0, 0)
     x_pass(2, 0, 1)
-    z_pass(0, 0)
-    x_own(0, 1)
-    z_pass(0, 1)
-    x_own(0, 2)
     x_end(0, 0)
     z_pass(1, 0)
     z_pass(1, 1)
-    x_end(1, 0)
+    x_pass(0, 1, 0)
+    x_pass(0, 1, 1)
     x_own(1, 1)
     tok_pass(1, 0, 0)
     tok_pass(1, 0, 1)
+    tok_second(1)
+    x_pass(0, 2, 0)
+    x_pass(0, 2, 1)
+    x_end(1, 0)
+    x_own(1, 2)
     x_end(2, 0)
-    tok_second(1)
-    x_own(1, 2)
-    x_pass(0, 1, 0)
-    x_pass(0, 1, 1)
+    x_end(0, 1)
     tok_pass(0, 0, 0)
     tok_pass(0, 0, 1)
-    x_pass(0, 2, 0)
     z_own(2)
+    z_end(0)
+    x_own(0, 3)
     tok_second(0)
-    x_pass(0, 2, 1)
     x_pass(1, 1, 0)
     x_pass(1, 1, 1)
+    x_end(0, 2)
+    tok_pass(1, 1, 1)
     x_pass(1, 2, 0)
-    tok_pass(1, 1, 1)
+    tok_pass(1, 1, 0)
     x_pass(1, 2, 1)
-    tok_pass(1, 1, 0)
-    z_end(0)
-    x_own(0, 3)
-    x_end(0, 1)
-    x_end(0, 2)
+    x_pass(0, 3, 0)
     z_end(1)
     x_own(1, 3)
+    x_pass(0, 3, 1)
     x_end(1, 1)
     z_pass(2, 1)
-    x_own(2, 2)
-    x_end(1, 2)
-    tok_pass(0, 1, 1)
     z_pass(2, 0)
     x_own(2, 1)
+    tok_pass(0, 1, 1)
+    x_end(1, 2)
     tok_pass(0, 1, 0)
-    x_pass(0, 3, 0)
-    x_pass(0, 3, 1)
+    x_own(2, 2)
     x_pass(1, 3, 0)
     x_pass(1, 3, 1)
-    x_pass(2, 2, 0)
-    x_pass(2, 2, 1)
+    x_end(0, 3)
     x_pass(2, 1, 0)
     x_pass(2, 1, 1)
     z_end(2)
     x_own(2, 3)
     tok_end(0)
     project_tokens(1 - core)
-    x_end(0, 3)
     x_end(1, 3)
-    x_end(2, 2)
+    x_pass(2, 2, 0)
+    x_pass(2, 2, 1)
     tok_end(1)
     project_tokens(core)
+    x_end(2, 1)
     x_pass(2, 3, 0)
     x_pass(2, 3, 1)
-    x_end(2, 1)
 
     def before(i):
+        if i == 1:
+            twin_end(0)
         if i == 2:
-            twin_end(0)
+            x_end(2, 2)
         if i == 4:
             x_end(2, 3)
-        if i == 6:
             twin_end(1)
-        if i == 8:
+        if i == 7:
             twin_end(2)
 
     def bias_of(slab, b, blk, lo, width):

time: 61.5 us -> 61 us (level)
  no operation moved by 1% of the time
where the time goes in v3:
time: 61 us; the launch traced here: 60.8 us
  Pallas kernels  59.1 us (97%)
  local copies, waits for them, and re-layouts  1.64 us (3%)
    pallas_call x1, Pallas kernels, shards(): pl.pallas_call(whole_kernel, out_shape=jax.ShapeDtypeStruct((2, TOK, D),...  59.1 us
    unnamed x1, local copies, waits for them, and re-layouts  1.64 us

profile of v3, /device:TPU:1, one launch (start us, length us, event | category | flops | bytes accessed | tf_op | source)
XLA Modules:
  0.0 60.8 jit_solution(15644964593397373415)
XLA Ops:
  0.0 59.1 %whole.1 = bf16[2,72,768]{2,1,0:T(8,128)(2,1)} custom-call(s32[72]{0:T(128)} %mask_ref.1, bf16[16,128]{1,0:T(8,128)(2,1)} %bitcast.1, s32[1152]{0:T(1024)} %token_ref.1, bf16[128,128]{1,0:T(8,128)(2,1)} %wq.1, bf16[128,128]{1,0:T(8,128)(2,1)} %wk.1, bf16[128,128]{1,0:T(8,128)(2,1)} %wv.1, bf16[128,128]{1,0:T(8,128)(2,1)} %wo.1, f32[768]{0:T(1024)} %gain_ref.1, ...), custom_call_target="tpu_custom_call" | custom-call | tf_op jit(solution)/shard_map/whole/pallas_call | solution.py:494
  59.2 1.6 %copy.18 = bf16[2,72,768]{2,1,0:T(8,128)(2,1)} copy(bf16[2,72,768]{2,1,0:T(8,128)(2,1)} %whole.1) | data formatting | bytes 442368

commit v4 on v3

--- a/solution.py
+++ b/solution.py
@@ -346,10 +346,13 @@
     pair_part(pair_load, pair_ref, mask_ref, pair_w_ref, table_ref, bias_ref.at[core, x % 2, zh, x // 2], row, col)
     loads[0].wait()
     loads[1].wait()
-    for s in (1 - core, core):
+
+    def inside(s):
         atom_project(s, feat_ref, wq[...], wk[...], wv[...], q_ref, k_ref, v_ref)
         for lo, hi in ((2, 14), (14, 26), (26, 34)):
             windows(s, range(lo, hi))
+
+    inside(1 - core)
 
     pl.semaphore_wait(barrier, 10)
     send(feat_hbm.at[:, ATOMS - RIM :], halo_ref.at[0], halo_send.at[0], halo_recv.at[0], r_up, col)
@@ -363,11 +366,12 @@
 
     z_own(0)
     x_own(0, 0)
+    z_own(1)
+    x_own(1, 0)
+    inside(core)
     counts_ref[...] = jnp.broadcast_to(token_counts(token_ref, row), (TOK, 128))
     loads[2].wait()
     inner(1 - core)
-    z_own(1)
-    x_own(1, 0)
     inner(core)
     for load in loads[3:]:
         load.wait()

time: 61 us -> 59.6 us (0.977)
  Pallas kernels: 59.1 us -> 57.8 us
    pallas_call x1, Pallas kernels: 59.1 us -> 57.8 us  [shards(): pl.pallas_call(whole_kernel, out_shape=jax.ShapeDtypeStruct((2, TOK, D),...]
where the time goes in v4:
time: 59.6 us; the launch traced here: 59.4 us
  Pallas kernels  57.8 us (97%)
  local copies, waits for them, and re-layouts  1.64 us (3%)
    pallas_call x1, Pallas kernels, shards(): pl.pallas_call(whole_kernel, out_shape=jax.ShapeDtypeStruct((2, TOK, D),...  57.8 us
    unnamed x1, local copies, waits for them, and re-layouts  1.64 us

profile of v4, /device:TPU:1, one launch (start us, length us, event | category | flops | bytes accessed | tf_op | source)
XLA Modules:
  0.0 59.4 jit_solution(4743559023698269490)
XLA Ops:
  0.0 57.8 %whole.1 = bf16[2,72,768]{2,1,0:T(8,128)(2,1)} custom-call(s32[72]{0:T(128)} %mask_ref.1, bf16[16,128]{1,0:T(8,128)(2,1)} %bitcast.1, s32[1152]{0:T(1024)} %token_ref.1, bf16[128,128]{1,0:T(8,128)(2,1)} %wq.1, bf16[128,128]{1,0:T(8,128)(2,1)} %wk.1, bf16[128,128]{1,0:T(8,128)(2,1)} %wv.1, bf16[128,128]{1,0:T(8,128)(2,1)} %wo.1, f32[768]{0:T(1024)} %gain_ref.1, ...), custom_call_target="tpu_custom_call" | custom-call | tf_op jit(solution)/shard_map/whole/pallas_call | solution.py:498
  57.8 1.6 %copy.18 = bf16[2,72,768]{2,1,0:T(8,128)(2,1)} copy(bf16[2,72,768]{2,1,0:T(8,128)(2,1)} %whole.1) | data formatting | bytes 442368
